TPU v7x, 32 devices: a whole 2x2x4 slice. The times are simulated.
32 devices in a mesh: dp: 8 (over z, y), seq: 4 (over x, core).
Axes of the slice: x: 2, y: 2, z: 4, core: 2. Of those that a mesh axis runs over, the one named last changes fastest.
Arguments:
- block_input: bfloat16 [8, 4, 256, 1408], P('dp', 'seq'), may hold values from -6 to 6
- norm_gain: float32 [1408], replicated, may hold values from 0.5 to 1.5
- qkv_weight: bfloat16 [1408, 4224], replicated, may hold values from -0.15625 to 0.15625
- frame_clip: int32 [8, 4], P('dp', 'seq'), may hold values from 0 to 2, never falling along the last dimension, each value on 1 to 2 neighbouring positions
- out_grad: bfloat16 [8, 4, 256, 1408], P('dp', 'seq'), may hold values from -6 to 6
Outputs:
- input_grad: bfloat16 [8, 4, 256, 1408], P('dp', 'seq')
- weight_grad: float32 [1408, 1408], P(('dp', 'seq'))
- gain_grad: float32 [1408], replicated
Inputs may be any that keep to these rules, and one draw needn't show every extreme that they name: `frame_clip`: in each group the frames hold clips 0 to 2 in order, each of 1 to 2 frames, one exactly 2.
All inputs are finite; a program needn't handle non-finite values.
Results may differ from a plain program's by a relative error of at most 0.018.
Values may be sent and summed in bfloat16 or wider, within the bound.
A program may use at most 128 MiB of HBM per device.

v0:
```python
import jax
import jax.numpy as jnp
from jax import lax
from jax.sharding import PartitionSpec as P

HEADS = 16


epsilon = 1e-06


def attention_grad(projected, incoming, same_clip):
    frames_all, positions, triple = projected.shape
    width = triple // 3
    head_dim = width // HEADS
    blocks = projected.reshape(frames_all, positions, 3, HEADS, head_dim)
    query_part = blocks[:, :, 0]
    key_part = blocks[:, :, 1]
    value_part = blocks[:, :, 2]
    outgrad = incoming.reshape(frames_all, positions, HEADS, head_dim)
    scaling = head_dim ** (-0.5)
    scores = (
        jnp.einsum("fphd,gphd->phfg", query_part, key_part, preferred_element_type=jnp.float32)
        * scaling
    )
    largest = jnp.max(jnp.where(same_clip, scores, -jnp.inf), axis=-1, keepdims=True)
    powers = jnp.where(same_clip, jnp.exp(scores - largest), 0.0)
    softmaxed = powers / jnp.sum(powers, axis=-1, keepdims=True)
    rounded_probs = softmaxed.astype(jnp.bfloat16)
    d_value = jnp.einsum(
        "phfg,fphd->gphd", rounded_probs, outgrad, preferred_element_type=jnp.float32
    )
    d_probs = jnp.einsum("fphd,gphd->phfg", outgrad, value_part, preferred_element_type=jnp.float32)
    row_dot = jnp.sum(softmaxed * d_probs, axis=-1, keepdims=True)
    d_scores = (softmaxed * (d_probs - row_dot) * scaling).astype(jnp.bfloat16)
    d_query = jnp.einsum("phfg,gphd->fphd", d_scores, key_part, preferred_element_type=jnp.float32)
    d_key = jnp.einsum("phfg,fphd->gphd", d_scores, query_part, preferred_element_type=jnp.float32)
    stacked = jnp.stack([d_query, d_key, d_value], axis=2)
    return stacked.reshape(frames_all, positions, triple).astype(jnp.bfloat16)


def transpose_product(grad_rows, qkv_weight):
    return lax.dot_general(
        grad_rows, qkv_weight, (((1,), (1,)), ((), ())), preferred_element_type=jnp.float32
    )


def shards(block_input, norm_gain, qkv_weight, frame_clip, out_grad):
    frames_dev = block_input.shape[1]
    patches = block_input.shape[2]
    width = block_input.shape[3]
    seq_count = lax.axis_size("seq")
    group_count = lax.axis_size("dp")
    local_pos = patches // seq_count
    factor = (frames_dev * patches * seq_count * group_count) ** (-0.5)
    inputs_f = block_input[0].astype(jnp.float32)
    centered = inputs_f - jnp.mean(inputs_f, axis=-1, keepdims=True)
    inv_std = lax.rsqrt(jnp.mean(centered * centered, axis=-1, keepdims=True) + epsilon)
    normalized = centered * inv_std
    normed = (normalized * norm_gain).astype(jnp.bfloat16)
    clip_ids = lax.all_gather(frame_clip, "seq", axis=1, tiled=True)[0]
    same_clip = clip_ids[:, None] == clip_ids[None, :]
    grad_split = out_grad[0].reshape(frames_dev, seq_count, local_pos, width)
    projected = jnp.dot(normed.reshape(-1, width), qkv_weight, preferred_element_type=jnp.float32)
    projected = projected.astype(jnp.bfloat16).reshape(frames_dev, seq_count, local_pos, 3 * width)
    moved_proj = lax.all_to_all(projected, "seq", split_axis=1, concat_axis=0, tiled=True)
    incoming = lax.all_to_all(grad_split, "seq", split_axis=1, concat_axis=0, tiled=True)
    grads_frames = attention_grad(moved_proj[:, 0], incoming[:, 0], same_clip)[:, None]
    grads_qkv = lax.all_to_all(grads_frames, "seq", split_axis=0, concat_axis=1, tiled=True)
    rows_x = normed.reshape(-1, width)
    rows_g = grads_qkv.reshape(-1, 3 * width)
    d_normed = transpose_product(rows_g, qkv_weight).reshape(frames_dev, patches, width)
    value_rows = rows_g[:, 2 * width :]
    weight_sum = lax.psum_scatter(
        lax.dot_general(
            rows_x, value_rows, (((0,), (0,)), ((), ())), preferred_element_type=jnp.float32
        ),
        ("dp", "seq"),
        scatter_dimension=0,
        tiled=True,
    )
    gain_local = jnp.sum(d_normed * normalized, axis=(0, 1))
    gain_sum = lax.psum(gain_local, ("dp", "seq"))
    d_hat = d_normed * norm_gain
    first_mean = jnp.mean(d_hat, axis=-1, keepdims=True)
    second_mean = jnp.mean(d_hat * normalized, axis=-1, keepdims=True)
    input_grad = (inv_std * (d_hat - first_mean - normalized * second_mean)).astype(jnp.bfloat16)
    return (input_grad[None], weight_sum * factor, gain_sum * factor)


def solution(mesh):
    placed = (P("dp", "seq", None, None), P(), P(), P("dp", "seq"), P("dp", "seq", None, None))
    return jax.shard_map(
        shards,
        mesh=mesh,
        in_specs=placed,
        out_specs=(P("dp", "seq", None, None), P(("dp", "seq"), None), P()),
        check_vma=False,
    )
```

profile of v0, /device:TPU:3, one launch (start us, length us, event | category | flops | bytes accessed | tf_op | source)
XLA Modules:
  0.0 278.5 jit_solution(6811882527229974068)
XLA Ops:
  0.6 0.0 copy-start
  0.6 0.0 copy-start.3
  0.7 3.8 %all-to-all-start.1 = ((bf16[1,4,64,1408]{3,2,0,1:T(8,128)(2,1)}), bf16[1,4,64,1408]{3,2,0,1:T(8,128)(2,1)S(1)}, u32[]{:S(2)}, u32[]{:S(2)}) async-start(bf16[1,4,64,1408]{3,2,0,1:T(8,128)(2,1)} %bitcast.102), calls=%async_computation.1 | async-start | bytes 1441792 | tf_op jit(solution)/shard_map/all_to_all | solution.py:67
  4.4 1.3 convert_reduce_fusion
  5.7 0.0 copy-done
  5.7 0.3 fusion.12
  6.0 0.0 copy-done.3
  6.1 9.5 %convolution_convert_fusion = bf16[256,4224]{1,0:T(8,128)(2,1)} fusion(bf16[1408,4224]{1,0:T(8,128)(2,1)} %param.7, bf16[1,1,256,1408]{3,2,1,0:T(8,128)(2,1)S(1)} %copy-done, f32[1408]{0:T(1024)S(1)} %copy-done.3, f32[256]{0:T(256)S(1)} %broadcast_multiply_fusion.3, f32[256]{0:T(256)S(1)} %add_rsqrt_fusion), kind=kOutput, calls=%fused_computation.2 | convolution fusion | flops 3047948288 | bytes 14786048 | tf_op jit(solution)/shard_map/dot_general | solution.py:64
  15.5 0.0 all-to-all-done.1
  15.5 0.0 copy-start.1
  15.5 0.0 copy-start.4
  15.5 0.9 copy-done.1
  16.4 3.6 %all-to-all-start = ((bf16[1,4,64,4224]{3,2,0,1:T(8,128)(2,1)}), bf16[1,4,64,4224]{3,2,0,1:T(8,128)(2,1)S(1)}, u32[]{:S(2)}, u32[]{:S(2)}) async-start(bf16[1,4,64,4224]{3,2,0,1:T(8,128)(2,1)} %bitcast.101), calls=%async_computation | async-start | bytes 4325376 | tf_op jit(solution)/shard_map/all_to_all | solution.py:66
  20.6 0.0 copy-done.4
  20.7 0.6 dynamic-slice
  21.2 0.7 bitcast_dynamic-update-slice_fusion
  21.9 22.7 %all-reduce = s32[4]{0:T(128)S(1)} all-reduce(s32[4]{0:T(128)S(1)} %bitcast_dynamic-update-slice_fusion), channel_id=1, replica_groups=mesh['dp'=8,'seq'=4] {'seq'}, use_global_device_ids=true, to_apply=%add | all-reduce | flops 4 | bytes 32 | tf_op jit(solution)/shard_map/eq | solution.py:62
  44.6 0.1 broadcast_compare_fusion
  44.7 3.9 %reshape_squeeze.11 = bf16[4,64,16,88]{3,2,1,0:T(8,128)(2,1)} reshape(bf16[1,4,64,1408]{3,2,0,1:T(8,128)(2,1)} %copy-done.1) | data formatting | bytes 1441792 | tf_op jit(solution)/shard_map/reshape;squeeze | solution.py:20
  48.6 0.0 all-to-all-done
  48.6 7.0 %reshape_squeeze.9 = bf16[4,64,3,16,88]{4,3,2,1,0:T(8,128)(2,1)} reshape(bf16[1,4,64,4224]{3,2,0,1:T(8,128)(2,1)S(1)} %all-to-all-done) | data formatting | bytes 4325376 | tf_op jit(solution)/shard_map/reshape;squeeze | solution.py:16
  55.6 2.5 fusion.44
  58.0 1.4 fusion.33
  59.5 0.0 copy-start.2
  59.5 3.4 %fusion.45 = (f32[64,16,4]{2,1,0:T(8,128)S(1)}, f32[64,16,4,4]{2,3,1,0:T(4,128)S(1)}) fusion(f32[64,16,4,4]{2,3,1,0:T(4,128)S(1)} %fusion.33, pred[4,4]{0,1:T(4,128)(4,1)S(1)} %broadcast_compare_fusion), kind=kOutput, calls=%fused_computation.65 | output fusion | flops 98307 | bytes 147472 | tf_op jit(solution)/shard_map/sub | solution.py:27
  62.9 0.0 copy-done.2
  62.9 1.5 fusion.28
  64.3 2.2 fusion.5
  66.6 1.9 fusion.25
  68.4 1.2 fusion.26
  69.7 1.3 fusion.27
  71.0 3.2 %pad_maximum_fusion = bf16[4,64,3,16,88]{4,0,3,1,2:T(4,128)(2,1)S(1)} fusion(bf16[4,64,1,16,88]{4,0,3,1,2:T(4,128)(2,1)S(1)} %fusion.27, bf16[4,64,1,16,88]{4,0,3,1,2:T(4,128)(2,1)S(1)} %fusion.26, bf16[4,64,1,16,88]{4,0,3,1,2:T(4,128)(2,1)S(1)} %fusion.25), kind=kLoop, calls=%fused_computation.3 | loop fusion | flops 2162688 | bytes 4325376 | tf_op jit(solution)/shard_map/stack | solution.py:38
  74.2 2.1 copy.23
  76.3 6.3 %convert_element_type.63 = bf16[4,1,64,4224]{3,2,0,1:T(8,128)(2,1)} reshape(bf16[4,64,3,16,88]{4,3,2,1,0:T(8,128)(2,1)} %copy.23) | data formatting | bytes 4325376 | tf_op jit(solution)/shard_map/convert_element_type | solution.py:39
  82.6 5.5 %all-to-all-start.2 = ((bf16[4,1,64,4224]{3,2,1,0:T(8,128)(2,1)}), bf16[4,1,64,4224]{3,2,1,0:T(8,128)(2,1)S(1)}, u32[]{:S(2)}, u32[]{:S(2)}) async-start(bf16[4,1,64,4224]{3,2,1,0:T(8,128)(2,1)} %bitcast.17), calls=%async_computation.2 | async-start | bytes 4325376 | tf_op jit(solution)/shard_map/all_to_all | solution.py:69
  88.0 24.5 %all-to-all-done.2 = bf16[4,1,64,4224]{3,2,1,0:T(8,128)(2,1)S(1)} async-done(((bf16[4,1,64,4224]{3,2,1,0:T(8,128)(2,1)}), bf16[4,1,64,4224]{3,2,1,0:T(8,128)(2,1)S(1)}, u32[]{:S(2)}, u32[]{:S(2)}) %all-to-all-start.2) | async-done | bytes 2162720 | tf_op jit(solution)/shard_map/all_to_all | solution.py:69
  112.5 4.6 %fusion.38 = f32[1408,1408]{1,0:T(8,128)} fusion(bf16[256,4224]{1,0:T(8,128)(2,1)S(1)} %bitcast.99, bf16[1,1,256,1408]{3,2,1,0:T(8,128)(2,1)S(1)} %copy-done, f32[1408]{0:T(1024)S(1)} %copy-done.3, f32[256]{0:T(256)S(1)} %broadcast_multiply_fusion.3, f32[256]{0:T(256)S(1)} %add_rsqrt_fusion), kind=kOutput, calls=%fused_computation.52 | convolution fusion | flops 1016823808 | bytes 9381888 | tf_op jit(solution)/shard_map/dot_general | solution.py:75
  117.1 96.4 %fusion = f32[48,1408]{1,0:T(8,128)S(1)} fusion(f32[1408,1408]{1,0:T(8,128)} %fusion.38), kind=kCustom, calls=%all-reduce-scatter | all-reduce-scatter fusion | flops 2162689 | bytes 8200192
  213.5 0.7 slice.20
  214.2 4.9 %collective-permute-start = (f32[48,1408]{1,0:T(8,128)S(1)}, f32[48,1408]{1,0:T(8,128)S(1)}, u32[]{:S(2)}, u32[]{:S(2)}) collective-permute-start(f32[48,1408]{1,0:T(8,128)S(1)} %fusion), channel_id=1, source_target_pairs={{0,1},{1,2},{2,3},{3,4},{4,5},{5,6},{6,7},{7,8},{8,9},{9,10},{10,1... | collective-permute-start | bytes 811016
  219.1 5.4 %collective-permute-start.1 = (f32[48,1408]{1,0:T(8,128)S(1)}, f32[48,1408]{1,0:T(8,128)}, u32[]{:S(2)}, u32[]{:S(2)}) collective-permute-start(f32[48,1408]{1,0:T(8,128)S(1)} %fusion), channel_id=1, source_target_pairs={{0,2},{1,3},{2,4},{3,5},{4,6},{5,7},{6,8},{7,9},{8,10},{9,11},{10,... | collective-permute-start | bytes 811016
  224.5 7.3 %fusion.24 = (f32[1408]{0:T(1024)S(1)}, f32[256]{0:T(256)S(1)}, f32[256]{0:T(256)S(1)}, f32[256,1408]{1,0:T(8,128)S(1)}) fusion(bf16[1,1,256,1408]{3,2,1,0:T(8,128)(2,1)S(1)} %copy-done, f32[256]{0:T(256)S(1)} %broadcast_multiply_fusion.3, f32[256]{0:T(256)S(1)} %add_rsqrt_fusion, f32[1408]{0:T(1024)S(1)} %copy-done.3, bf16[256,4224]{1,0:T(8,128)(2,1)S(1)} %bitcast.100, ...), kind=kOutput, calls=%fused_computation.33 | convolution fusion | flops 3048306688 | bytes 16235520 | tf_op jit(solution)/shard_map/dot_general | solution.py:43
  231.8 1.9 collective-permute-start.2
  233.8 1.3 fusion.37
  235.1 40.5 %psum.7 = f32[1408]{0:T(1024)S(1)} all-reduce(f32[1408]{0:T(1024)S(1)} %get-tuple-element.3), channel_id=1, replica_groups=mesh['dp'=8,'seq'=4] {'dp','seq'}, use_global_device_ids=true, to_apply=%region_9.10 | all-reduce | flops 1408 | bytes 11264 | tf_op jit(solution)/shard_map/psum | solution.py:83
  275.6 0.6 broadcast_multiply_fusion
  276.2 0.0 collective-permute-done.2
  276.3 0.0 collective-permute-done
  276.3 0.0 collective-permute-done.1
  276.3 1.5 concatenate
  277.8 0.7 dynamic-slice_multiply_fusion
  (4 shorter events, 0.0 us)
Async XLA Ops:
  0.6 5.1 %copy-start = (bf16[1,1,256,1408]{3,2,1,0:T(8,128)(2,1)S(1)}, bf16[1,1,256,1408]{3,2,1,0:T(8,128)(2,1)}, u32[]{:S(2)}) copy-start(bf16[1,1,256,1408]{3,2,1,0:T(8,128)(2,1)} %param.5) | copy-start | bytes 2162692
  0.6 5.4 %copy-start.3 = (f32[1408]{0:T(1024)S(1)}, f32[1408]{0:T(1024)}, u32[]{:S(2)}) copy-start(f32[1408]{0:T(1024)} %param.6) | copy-start | bytes 16900
  0.7 14.9 %all-to-all-start.1 = ((bf16[1,4,64,1408]{3,2,0,1:T(8,128)(2,1)}), bf16[1,4,64,1408]{3,2,0,1:T(8,128)(2,1)S(1)}, u32[]{:S(2)}, u32[]{:S(2)}) async-start(bf16[1,4,64,1408]{3,2,0,1:T(8,128)(2,1)} %bitcast.102), calls=%async_computation.1 | async-start | bytes 1441792 | tf_op jit(solution)/shard_map/all_to_all | solution.py:67
  15.5 0.9 copy-start.1
  15.5 5.1 %copy-start.4 = (u32[32]{0:T(128)S(1)}, u32[32]{0:T(128)}, u32[]{:S(2)}) copy-start(u32[32]{0:T(128)} %constant.22) | copy-start | bytes 388
  16.4 32.2 %all-to-all-start = ((bf16[1,4,64,4224]{3,2,0,1:T(8,128)(2,1)}), bf16[1,4,64,4224]{3,2,0,1:T(8,128)(2,1)S(1)}, u32[]{:S(2)}, u32[]{:S(2)}) async-start(bf16[1,4,64,4224]{3,2,0,1:T(8,128)(2,1)} %bitcast.101), calls=%async_computation | async-start | bytes 4325376 | tf_op jit(solution)/shard_map/all_to_all | solution.py:66
  59.5 3.4 %copy-start.2 = (bf16[4,64,16,88]{3,2,1,0:T(8,128)(2,1)S(1)}, bf16[4,64,16,88]{3,2,1,0:T(8,128)(2,1)}, u32[]{:S(2)}) copy-start(bf16[4,64,16,88]{3,2,1,0:T(8,128)(2,1)} %reshape_squeeze.11) | copy-start | bytes 2162692
  82.6 30.0 %all-to-all-start.2 = ((bf16[4,1,64,4224]{3,2,1,0:T(8,128)(2,1)}), bf16[4,1,64,4224]{3,2,1,0:T(8,128)(2,1)S(1)}, u32[]{:S(2)}, u32[]{:S(2)}) async-start(bf16[4,1,64,4224]{3,2,1,0:T(8,128)(2,1)} %bitcast.17), calls=%async_computation.2 | async-start | bytes 4325376 | tf_op jit(solution)/shard_map/all_to_all | solution.py:69
  214.2 62.0 %collective-permute-start = (f32[48,1408]{1,0:T(8,128)S(1)}, f32[48,1408]{1,0:T(8,128)S(1)}, u32[]{:S(2)}, u32[]{:S(2)}) collective-permute-start(f32[48,1408]{1,0:T(8,128)S(1)} %fusion), channel_id=1, source_target_pairs={{0,1},{1,2},{2,3},{3,4},{4,5},{5,6},{6,7},{7,8},{8,9},{9,10},{10,1... | collective-permute-start | bytes 811016
  219.1 57.1 %collective-permute-start.1 = (f32[48,1408]{1,0:T(8,128)S(1)}, f32[48,1408]{1,0:T(8,128)}, u32[]{:S(2)}, u32[]{:S(2)}) collective-permute-start(f32[48,1408]{1,0:T(8,128)S(1)} %fusion), channel_id=1, source_target_pairs={{0,2},{1,3},{2,4},{3,5},{4,6},{5,7},{6,8},{7,9},{8,10},{9,11},{10,... | collective-permute-start | bytes 811016
  231.8 44.4 %collective-permute-start.2 = (f32[28,1408]{1,0:T(8,128)}, f32[28,1408]{1,0:T(8,128)S(1)}, u32[]{:S(2)}, u32[]{:S(2)}) collective-permute-start(f32[28,1408]{1,0:T(8,128)} %slice.20), channel_id=1, source_target_pairs={{0,3},{1,4},{2,5},{3,6},{4,7},{5,8},{6,9},{7,10},{8,11},{9,12},{10... | collective-permute-start | bytes 473096
where the time goes:
time: 281 us; the launch traced here: 279 us
  blocking collectives  160 us (57%)
  matrix products  28.7 us (10%)
  local copies, waits for them, and re-layouts  26 us (9%)
  starting transfers between devices  25.1 us (9%)
  waiting for transfers between devices  24.5 us (9%)
  other arithmetic  13.2 us (5%)
    unnamed x1, blocking collectives  96.4 us
    psum x1, blocking collectives, shards(): gain_sum = lax.psum(gain_local, ('dp', 'seq'))  40.5 us
    all_to_all x1, waiting for transfers between devices, shards(): lax.all_to_all(grads_frames, 'seq', split_axis=0, concat_axis=1, tiled=True)  24.5 us
    eq x1, blocking collectives, shards(): same_clip = clip_ids[:, None] == clip_ids[None, :]  22.7 us
    unnamed x3, starting transfers between devices  12.2 us
    dot_general x1, matrix products, shards(): jnp.dot(normed.reshape(-1, width), qkv_weight, preferred_element_type=jnp...  9.46 us
    dot_general x1, matrix products, transpose_product(): lax.dot_general(grad_rows, qkv_weight, (((1,), (1,)), ((), ())), preferre...  7.3 us
    another operation x1, local copies, waits for them, and re-layouts, attention_grad(): blocks = projected.reshape(frames_all, positions, 3, HEADS, head_dim)  6.99 us
  transfers between devices with their start and end apart: 6, of which 1 were waited for; matrix products, arithmetic and copies ran while one was open for 9% of the time, Pallas kernels for 0%

commit v1 on v0

--- a/solution.py
+++ b/solution.py
@@ -1,6 +1,8 @@
 import jax
 import jax.numpy as jnp
 from jax import lax
+from jax.experimental import pallas as pl
+from jax.experimental.pallas import tpu as pltpu
 from jax.sharding import PartitionSpec as P
 
 HEADS = 16
@@ -88,12 +90,439 @@
     return (input_grad[None], weight_sum * factor, gain_sum * factor)
 
 
+MESH = pl.DeviceIdType.MESH
+BF = jnp.bfloat16
+F32 = jnp.float32
+ROWS = 16
+PAD = 48
+SPLIT = 768
+
+
+def fused(
+    x_ref, do_ref, gain_ref, w_hbm, clip_ref,
+    ig_ref, wg_ref, gg_ref,
+    w, rn, rp, cn, cp, mk, nz, iv, nb, dos, proj, t1, t2, em, et, bc, g, dn, igs, qn, qp,
+    tr, nt, nr, dvr, sx, sy, rx, ry, kx, ky, tx, ty, rtx, rty, fin, u, zr, gp, gr, zg,
+    wsem, send, recv,
+):
+    dp = lax.axis_index("dp")
+    s = lax.axis_index("seq")
+    z, y = dp // 2, dp % 2
+    xx, core = s // 2, s % 2
+    half = x_ref.shape[0] // 2
+    width = x_ref.shape[1]
+    head_dim = width // HEADS
+    block = wg_ref.shape[0]
+    scaling = head_dim ** (-0.5)
+    prev, after = (dp, lax.rem(s + 3, 4)), (dp, lax.rem(s + 1, 4))
+    has_prev, has_next = s > 0, s < 3
+    core_dev = (dp, xx * 2 + (1 - core))
+    x_dev = (dp, (1 - xx) * 2 + core)
+    y_dev = (z * 2 + (1 - y), s)
+    z_devs = [(lax.rem(z + d, 4) * 2 + y, s) for d in (1, 2, 3)]
+
+    loads = [
+        pltpu.make_async_copy(w_hbm.at[:, pl.ds(j * width, width)], w.at[j], wsem.at[j])
+        for j in range(3)
+    ]
+    for load in loads:
+        load.start()
+
+    barrier = pltpu.get_barrier_semaphore()
+    for dev in [core_dev, x_dev, y_dev, (dp, 3 - s)] + z_devs:
+        pl.semaphore_signal(barrier, inc=1, device_id=dev, device_id_type=MESH)
+    pl.semaphore_wait(barrier, 7)
+
+    def remote(index, src, dst, dev):
+        return pltpu.make_async_remote_copy(
+            src_ref=src, dst_ref=dst, send_sem=send.at[index], recv_sem=recv.at[index],
+            device_id=dev, device_id_type=MESH,
+        )
+
+    lower, upper = pl.ds(0, half), pl.ds(half, half)
+    clip_p = remote(4, clip_ref, cn, prev)
+    clip_n = remote(5, clip_ref, cp, after)
+    x_p = remote(0, x_ref.at[lower], rn.at[0], prev)
+    do_p = remote(1, do_ref.at[lower], rn.at[1], prev)
+    x_n = remote(2, x_ref.at[upper], rp.at[0], after)
+    do_n = remote(3, do_ref.at[upper], rp.at[1], after)
+    to_prev, to_next = [clip_p, x_p, do_p], [clip_n, x_n, do_n]
+
+    @pl.when(has_prev)
+    def _():
+        for copy in to_prev:
+            copy.start()
+
+    @pl.when(has_next)
+    def _():
+        for copy in to_next:
+            copy.start()
+
+    @pl.when(s == 0)
+    def _():
+        rp[...] = jnp.zeros_like(rp)
+        cp[...] = jnp.full_like(cp, -1.0)
+
+    @pl.when(s == 3)
+    def _():
+        rn[...] = jnp.zeros_like(rn)
+        cn[...] = jnp.full_like(cn, -1.0)
+
+    row = lax.broadcasted_iota(jnp.int32, em.shape, 0)
+    col = lax.broadcasted_iota(jnp.int32, em.shape, 1) * head_dim
+    em[...] = jnp.where((row >= col) & (row < col + head_dim), 1.0, 0.0).astype(BF)
+    row = lax.broadcasted_iota(jnp.int32, et.shape, 0) * head_dim
+    col = lax.broadcasted_iota(jnp.int32, et.shape, 1)
+    et[...] = jnp.where((col >= row) & (col < row + head_dim), 1.0, 0.0).astype(BF)
+    tr[pl.ds(width, 8), :] = jnp.zeros((8, tr.shape[1]), F32)
+
+    @pl.when(has_next)
+    def _():
+        clip_p.wait_recv()
+        x_p.wait_recv()
+
+    @pl.when(has_prev)
+    def _():
+        clip_n.wait_recv()
+        x_n.wait_recv()
+
+    own_clip = clip_ref[...]
+    mk[0] = jnp.where(own_clip == cp[...], 1.0, 0.0)
+    mk[1] = jnp.where(own_clip == cn[...], 1.0, 0.0)
+
+    def masks(shape):
+        before = jnp.broadcast_to(mk[0, 0:1, 0:1], shape) > 0.5
+        later = jnp.broadcast_to(mk[1, 0:1, 0:1], shape) > 0.5
+        return before, later
+
+    def pick(own, index, r):
+        before, later = masks((ROWS, width))
+        lo = own[pl.ds(r, ROWS), :].astype(F32)
+        hi = own[pl.ds(half + r, ROWS), :].astype(F32)
+        from_next = rn[index, pl.ds(r, ROWS), :].astype(F32)
+        from_prev = rp[index, pl.ds(r, ROWS), :].astype(F32)
+        first = jnp.where(before, hi, lo)
+        second = jnp.where(later, from_next, jnp.where(before, from_prev, hi))
+        return first, second
+
+    chunks = half // ROWS
+
+    def norm_rows(c, carry):
+        r = pl.multiple_of(c * ROWS, ROWS)
+        for base, rows in zip((0, half), pick(x_ref, 0, r)):
+            at = pl.ds(base + r, ROWS)
+            centered = rows - jnp.mean(rows, axis=-1, keepdims=True)
+            inv = lax.rsqrt(jnp.mean(centered * centered, axis=-1, keepdims=True) + epsilon)
+            normalized = centered * inv
+            nz[at, :] = normalized
+            iv[at, :] = jnp.broadcast_to(inv, (ROWS, 128))
+            nb[at, :] = (normalized * gain_ref[...]).astype(BF)
+        return carry
+
+    lax.fori_loop(0, chunks, norm_rows, 0)
+
+    for j in range(3):
+        loads[j].wait()
+
+    def project(j, carry):
+        proj[j] = jnp.dot(nb[...], w[j], preferred_element_type=F32).astype(BF)
+        return carry
+
+    lax.fori_loop(0, 3, project, 0)
+
+    tr[pl.ds(0, width), :] = jnp.transpose(nb[...].astype(F32))
+    for i in range(32):
+        nt[i % 2, (i // 2) % 2 * 2 + (i // 4) % 2, pl.ds(i // 8 * PAD, PAD), :] = tr[
+            pl.ds(i * block, PAD), :
+        ].astype(BF)
+    nt_copy = remote(6, nt.at[1 - core], nr, core_dev)
+    nt_copy.start()
+
+    @pl.when(has_next)
+    def _():
+        do_p.wait_recv()
+
+    @pl.when(has_prev)
+    def _():
+        do_n.wait_recv()
+
+    def products(c, carry):
+        r = pl.multiple_of(c * ROWS, ROWS)
+        a, b = pl.ds(r, ROWS), pl.ds(half + r, ROWS)
+        do_a, do_b = pick(do_ref, 1, r)
+        dos[a, :] = do_a.astype(BF)
+        dos[b, :] = do_b.astype(BF)
+        kd = proj[1, a, :].astype(F32) - proj[1, b, :].astype(F32)
+        vd = proj[2, a, :].astype(F32) - proj[2, b, :].astype(F32)
+        t1[a, :] = (proj[0, a, :].astype(F32) * kd).astype(BF)
+        t1[b, :] = (proj[0, b, :].astype(F32) * -kd).astype(BF)
+        t2[a, :] = (do_a * vd).astype(BF)
+        t2[b, :] = (do_b * -vd).astype(BF)
+        return carry
+
+    lax.fori_loop(0, chunks, products, 0)
+
+    sd = jnp.dot(t1[...], em[...], preferred_element_type=F32) * scaling
+    dd = jnp.dot(t2[...], em[...], preferred_element_type=F32)
+    before, later = masks(sd.shape)
+    paired = before | later
+    own_p = jnp.where(paired, 1.0 / (1.0 + jnp.exp(-sd)), 1.0)
+    other_p = jnp.where(paired, 1.0 / (1.0 + jnp.exp(sd)), 0.0)
+    ds = own_p * other_p * dd * scaling
+    for j, small in enumerate((own_p, other_p, ds)):
+        bc[j] = jnp.dot(small.astype(BF), et[...], preferred_element_type=F32).astype(BF)
+
+    def value_rows(c, carry):
+        r = pl.multiple_of(c * ROWS, ROWS)
+        a, b = pl.ds(r, ROWS), pl.ds(half + r, ROWS)
+        do_a, do_b = dos[a, :].astype(F32), dos[b, :].astype(F32)
+        g[2, a, :] = (bc[0, a, :].astype(F32) * do_a + bc[1, b, :].astype(F32) * do_b).astype(BF)
+        g[2, b, :] = (bc[0, b, :].astype(F32) * do_b + bc[1, a, :].astype(F32) * do_a).astype(BF)
+        return carry
+
+    lax.fori_loop(0, chunks, value_rows, 0)
+    dv_copy = remote(7, g.at[2], dvr, core_dev)
+    dv_copy.start()
+
+    def grad_rows(c, carry):
+        r = pl.multiple_of(c * ROWS, ROWS)
+        a, b = pl.ds(r, ROWS), pl.ds(half + r, ROWS)
+        ds_a, ds_b = bc[2, a, :].astype(F32), bc[2, b, :].astype(F32)
+        kd = proj[1, a, :].astype(F32) - proj[1, b, :].astype(F32)
+        g[0, a, :] = (ds_a * kd).astype(BF)
+        g[0, b, :] = (ds_b * -kd).astype(BF)
+        dk = ds_a * proj[0, a, :].astype(F32) - ds_b * proj[0, b, :].astype(F32)
+        g[1, a, :] = dk.astype(BF)
+        g[1, b, :] = (-dk).astype(BF)
+        return carry
+
+    lax.fori_loop(0, chunks, grad_rows, 0)
+
+    nt_copy.wait_recv()
+    dv_copy.wait_recv()
+
+    def term(group, cols):
+        return jnp.dot(nt[core, group], g[2, :, cols], preferred_element_type=F32) + jnp.dot(
+            nr[group], dvr[:, cols], preferred_element_type=F32
+        )
+
+    cols_y, cols_x = pl.ds(0, SPLIT), pl.ds(SPLIT, width - SPLIT)
+
+    def send_terms(k, carry):
+        sx[k] = term((1 - xx) * 2 + k, cols_x).astype(BF)
+        sy[k] = term(k * 2 + (1 - y), cols_y).astype(BF)
+        return carry
+
+    lax.fori_loop(0, 2, send_terms, 0)
+    x_first = remote(10, sx, rx, x_dev)
+    y_first = remote(11, sy, ry, y_dev)
+    x_first.start()
+    y_first.start()
+
+    def back(j, carry):
+        part = lax.dot_general(
+            g[j], w[j], (((1,), (1,)), ((), ())), preferred_element_type=F32
+        )
+        dn[...] = dn[...] + part
+        return carry
+
+    dn[...] = jnp.zeros_like(dn)
+    lax.fori_loop(0, 3, back, 0)
+
+    def input_rows(c, acc):
+        r = pl.multiple_of(c * ROWS, ROWS)
+        at = pl.ds(r, ROWS)
+        normalized, d_normed = nz[at, :], dn[at, :]
+        prod = d_normed * normalized
+        d_hat = d_normed * gain_ref[...]
+        first = jnp.mean(d_hat, axis=-1, keepdims=True)
+        second = jnp.mean(d_hat * normalized, axis=-1, keepdims=True)
+        result = iv[at, 0:1] * (d_hat - first - normalized * second)
+        igs[at, :] = result.astype(BF)
+        return acc + (prod[0:8] + prod[8:16])
+
+    gp[0] = lax.fori_loop(0, 2 * chunks, input_rows, jnp.zeros((8, width), F32))
+
+    ig_p = remote(8, igs.at[upper], qn, prev)
+    ig_n = remote(9, igs.at[upper], qp, after)
+
+    @pl.when(has_prev)
+    def _():
+        ig_p.start()
+
+    @pl.when(has_next)
+    def _():
+        ig_n.start()
+
+    @pl.when(s == 0)
+    def _():
+        qp[...] = jnp.zeros_like(qp)
+
+    @pl.when(s == 3)
+    def _():
+        qn[...] = jnp.zeros_like(qn)
+
+    gain_core = remote(17, gp.at[0], gr.at[0], core_dev)
+    gain_core.start()
+
+    def keep_terms(k, carry):
+        kx[k] = term(xx * 2 + k, cols_x)
+        ky[k] = term(k * 2 + y, cols_y)
+        return carry
+
+    lax.fori_loop(0, 2, keep_terms, 0)
+
+    gain_core.wait_recv()
+    gp[1] = gp[0] + gr[0]
+    gain_x = remote(18, gp.at[1], gr.at[1], x_dev)
+    gain_x.start()
+
+    y_first.wait_recv()
+    tx[...] = (ky[1 - xx] + ry[1 - xx].astype(F32)).astype(BF)
+    x_second = remote(12, tx, rtx, x_dev)
+    x_second.start()
+    x_first.wait_recv()
+    ty[...] = (kx[1 - y] + rx[1 - y].astype(F32)).astype(BF)
+    y_second = remote(13, ty, rty, y_dev)
+    y_second.start()
+
+    gain_x.wait_recv()
+    gp[2] = gp[1] + gr[1]
+    gain_y = remote(19, gp.at[2], gr.at[2], y_dev)
+    gain_y.start()
+
+    fin[:, cols_y] = ky[xx] + ry[xx].astype(F32)
+    fin[:, cols_x] = kx[y] + rx[y].astype(F32)
+
+    gain_y.wait_recv()
+    zg[z] = gp[2] + gr[2]
+    gain_z = [remote(20 + d, zg.at[z], zg.at[z], z_devs[d]) for d in range(3)]
+    for copy in gain_z:
+        copy.start()
+
+    @pl.when(has_next)
+    def _():
+        ig_p.wait_recv()
+
+    @pl.when(has_prev)
+    def _():
+        ig_n.wait_recv()
+
+    def output_rows(c, carry):
+        r = pl.multiple_of(c * ROWS, ROWS)
+        a, b = pl.ds(r, ROWS), pl.ds(half + r, ROWS)
+        prior, later_too = masks((ROWS, width))
+        first, second = igs[a, :].astype(F32), igs[b, :].astype(F32)
+        ig_ref[a, :] = jnp.where(prior, qp[a, :].astype(F32), first).astype(BF)
+        ig_ref[b, :] = jnp.where(
+            prior, first, jnp.where(later_too, qn[a, :].astype(F32), second)
+        ).astype(BF)
+        return carry
+
+    lax.fori_loop(0, chunks, output_rows, 0)
+
+    x_second.wait_recv()
+    fin[:, cols_y] = fin[:, cols_y] + rtx[...].astype(F32)
+    y_second.wait_recv()
+    fin[:, cols_x] = fin[:, cols_x] + rty[...].astype(F32)
+    for k in range(4):
+        u[k] = fin[pl.ds(k * PAD, PAD), :].astype(BF)
+    z_copies = [
+        remote(14 + d, u.at[lax.rem(z + d + 1, 4)], zr.at[d], z_devs[d]) for d in range(3)
+    ]
+    for copy in z_copies:
+        copy.start()
+
+    factor = (x_ref.shape[0] * 32) ** (-0.5)
+    for copy in gain_z:
+        copy.wait_recv()
+    total = (zg[0] + zg[1]) + (zg[2] + zg[3])
+    gg_ref[...] = jnp.sum(total, axis=0, keepdims=True) * factor
+
+    for copy in z_copies:
+        copy.wait_recv()
+    own = fin[pl.ds(pl.multiple_of(z * PAD, PAD), PAD), :]
+    summed = own + zr[0].astype(F32) + zr[1].astype(F32) + zr[2].astype(F32)
+    wg_ref[...] = summed[0:block] * factor
+
+    @pl.when(has_prev)
+    def _():
+        for copy in to_prev + [ig_p]:
+            copy.wait_send()
+
+    @pl.when(has_next)
+    def _():
+        for copy in to_next + [ig_n]:
+            copy.wait_send()
+
+    sent = [nt_copy, dv_copy, x_first, y_first, x_second, y_second, gain_core, gain_x, gain_y]
+    for copy in sent + gain_z + z_copies:
+        copy.wait_send()
+
+
+def paired_shards(block_input, norm_gain, qkv_weight, frame_clip, out_grad):
+    tokens, width = block_input.shape[2:]
+    half = tokens // 2
+    block = width // 32
+    clip = jnp.broadcast_to(frame_clip.astype(F32), (8, 128))
+    vmem = pl.BlockSpec(memory_space=pltpu.VMEM)
+    rest = width - SPLIT
+    group = 4 * PAD
+
+    def buf(*shape):
+        return pltpu.VMEM(shape, BF)
+
+    def wide(*shape):
+        return pltpu.VMEM(shape, F32)
+
+    scratch = [
+        buf(3, width, width), buf(2, half, width), buf(2, half, width),
+        wide(8, 128), wide(8, 128), wide(2, 8, 128),
+        wide(tokens, width), wide(tokens, 128), buf(tokens, width), buf(tokens, width),
+        buf(3, tokens, width), buf(tokens, width), buf(tokens, width),
+        buf(width, 128), buf(128, width), buf(3, tokens, width), buf(3, tokens, width),
+        wide(tokens, width), buf(tokens, width), buf(half, width), buf(half, width),
+        wide(width + 8, tokens), buf(2, 4, group, tokens), buf(4, group, tokens),
+        buf(tokens, width),
+        buf(2, group, rest), buf(2, group, SPLIT), buf(2, group, rest), buf(2, group, SPLIT),
+        wide(2, group, rest), wide(2, group, SPLIT),
+        buf(group, SPLIT), buf(group, rest), buf(group, SPLIT), buf(group, rest),
+        wide(group, width), buf(4, PAD, width), buf(3, PAD, width),
+        wide(3, 8, width), wide(3, 8, width), wide(4, 8, width),
+        pltpu.SemaphoreType.DMA((3,)),
+        pltpu.SemaphoreType.DMA((23,)), pltpu.SemaphoreType.DMA((23,)),
+    ]
+    input_grad, weight_grad, gain_grad = pl.pallas_call(
+        fused,
+        out_shape=(
+            jax.ShapeDtypeStruct((tokens, width), BF),
+            jax.ShapeDtypeStruct((block, width), F32),
+            jax.ShapeDtypeStruct((1, width), F32),
+        ),
+        in_specs=[vmem, vmem, vmem, pl.BlockSpec(memory_space=pl.ANY), vmem],
+        out_specs=(vmem, vmem, vmem),
+        scratch_shapes=scratch,
+        compiler_params=pltpu.CompilerParams(
+            collective_id=0, has_side_effects=True, vmem_limit_bytes=56 * 1024 * 1024
+        ),
+        cost_estimate=pl.CostEstimate(
+            flops=8_000_000_000, bytes_accessed=16_000_000, transcendentals=100_000
+        ),
+    )(block_input[0, 0], out_grad[0, 0], norm_gain[None], qkv_weight, clip)
+    return input_grad[None, None], weight_grad, gain_grad[0]
+
+
 def solution(mesh):
     placed = (P("dp", "seq", None, None), P(), P(), P("dp", "seq"), P("dp", "seq", None, None))
-    return jax.shard_map(
-        shards,
-        mesh=mesh,
-        in_specs=placed,
-        out_specs=(P("dp", "seq", None, None), P(("dp", "seq"), None), P()),
-        check_vma=False,
-    )
+
+    def whole(block_input, *others):
+        small = mesh.shape["dp"] == 8 and mesh.shape["seq"] == 4 and block_input.shape[1] == 4
+        return jax.shard_map(
+            paired_shards if small else shards,
+            mesh=mesh,
+            in_specs=placed,
+            out_specs=(P("dp", "seq", None, None), P(("dp", "seq"), None), P()),
+            check_vma=False,
+        )(block_input, *others)
+
+    return whole

time: 281 us -> 69.7 us (0.25)
  the two profiles are of different devices: /device:TPU:3 before, /device:TPU:14 now
where the time goes in v1:
time: 69.7 us; the launch traced here: 69.4 us
  Pallas kernels  61.2 us (88%)
  local copies, waits for them, and re-layouts  5.58 us (8%)
  other arithmetic  1.31 us (2%)
  between operations  1.29 us (2%)
    pallas_call x1, Pallas kernels, paired_shards(): pl.pallas_call(fused, out_shape=(jax.ShapeDtypeStruct((tokens, width), BF...  61.2 us
    unnamed x2, local copies, waits for them, and re-layouts  3.69 us

profile of v1, /device:TPU:14, one launch (start us, length us, event | category | flops | bytes accessed | tf_op | source)
XLA Modules:
  0.0 69.4 jit_solution(7328491033308007066)
XLA Ops:
  1.3 0.6 broadcast_in_dim.15.clip_ref
  1.9 1.3 %broadcast_in_dim.13.gain_ref = f32[1,1408]{1,0:T(1,128)} reshape(f32[1408]{0:T(1024)} %param.6) | data formatting | bytes 11264 | tf_op jit(solution)/shard_map/broadcast_in_dim | solution.py:511
  3.2 61.2 %shard_map.76 = (bf16[256,1408]{1,0:T(8,128)(2,1)}, f32[44,1408]{1,0:T(8,128)}, f32[1,1408]{1,0:T(1,128)}) custom-call(bf16[256,1408]{1,0:T(8,128)(2,1)} %bitcast.5, bf16[256,1408]{1,0:T(8,128)(2,1)} %bitcast.6, f32[1,1408]{1,0:T(1,128)} %broadcast_in_dim.13.gain_ref, bf16[1408,4224]{1,0:T(8,128)(2,1)} %w_hbm.1, f32[8,128]{1,0:T(8,128)} %broadcast_in_dim.15.clip_ref), custom_call_target="tpu_custom_call" | custom-call | flops 8000000000 | bytes 16000000 | tf_op jit(solution)/shard_map/pallas_call | solution.py:495
  64.4 1.3 %reduce = f32[1408]{0:T(1024)} reduce(f32[1,1408]{1,0:T(1,128)} %get-tuple-element.8, f32[]{:T(128)} %constant.3), dimensions={0}, to_apply=%get-tuple-element.8.reduce_sub_computation | reduce | bytes 11268 | tf_op jit(solution)/shard_map/pallas_call | solution.py:495
  65.7 2.0 %copy.11 = bf16[1,1,256,1408]{3,2,1,0:T(8,128)(2,1)} copy(bf16[1,1,256,1408]{3,2,1,0:T(8,128)(2,1)} %bitcast.4) | data formatting | bytes 1441792
  67.7 1.7 %copy.12 = f32[44,1408]{1,0:T(8,128)} copy(f32[44,1408]{1,0:T(8,128)} %get-tuple-element.13) | data formatting | bytes 495616

commit v2 on v1

--- a/solution.py
+++ b/solution.py
@@ -95,13 +95,16 @@
 F32 = jnp.float32
 ROWS = 16
 PAD = 48
-SPLIT = 768
+SPLIT = 896
+PARTS_Y = ((0, 384), (384, 256), (640, 256))
+PARTS_X = ((0, 256), (256, 128), (384, 128))
+CHUNKS = range(3)
 
 
 def fused(
     x_ref, do_ref, gain_ref, w_hbm, clip_ref,
     ig_ref, wg_ref, gg_ref,
-    w, rn, rp, cn, cp, mk, nz, iv, nb, dos, proj, t1, t2, em, et, bc, g, dn, igs, qn, qp,
+    gn, cl, w, rn, rp, cn, cp, mk, nz, iv, nb, dos, proj, t1, t2, em, et, bc, g, dn, igs, qn, qp,
     tr, nt, nr, dvr, sx, sy, rx, ry, kx, ky, tx, ty, rtx, rty, fin, u, zr, gp, gr, zg,
     wsem, send, recv,
 ):
@@ -128,6 +131,9 @@
     for load in loads:
         load.start()
 
+    gn[...] = gain_ref[...].reshape(1, width)
+    cl[...] = jnp.full(cl.shape, clip_ref[0, 0], jnp.int32)
+
     barrier = pltpu.get_barrier_semaphore()
     for dev in [core_dev, x_dev, y_dev, (dp, 3 - s)] + z_devs:
         pl.semaphore_signal(barrier, inc=1, device_id=dev, device_id_type=MESH)
@@ -140,8 +146,8 @@
         )
 
     lower, upper = pl.ds(0, half), pl.ds(half, half)
-    clip_p = remote(4, clip_ref, cn, prev)
-    clip_n = remote(5, clip_ref, cp, after)
+    clip_p = remote(4, cl, cn, prev)
+    clip_n = remote(5, cl, cp, after)
     x_p = remote(0, x_ref.at[lower], rn.at[0], prev)
     do_p = remote(1, do_ref.at[lower], rn.at[1], prev)
     x_n = remote(2, x_ref.at[upper], rp.at[0], after)
@@ -161,12 +167,12 @@
     @pl.when(s == 0)
     def _():
         rp[...] = jnp.zeros_like(rp)
-        cp[...] = jnp.full_like(cp, -1.0)
+        cp[...] = jnp.full_like(cp, -1)
 
     @pl.when(s == 3)
     def _():
         rn[...] = jnp.zeros_like(rn)
-        cn[...] = jnp.full_like(cn, -1.0)
+        cn[...] = jnp.full_like(cn, -1)
 
     row = lax.broadcasted_iota(jnp.int32, em.shape, 0)
     col = lax.broadcasted_iota(jnp.int32, em.shape, 1) * head_dim
@@ -179,14 +185,12 @@
     @pl.when(has_next)
     def _():
         clip_p.wait_recv()
-        x_p.wait_recv()
 
     @pl.when(has_prev)
     def _():
         clip_n.wait_recv()
-        x_n.wait_recv()
-
-    own_clip = clip_ref[...]
+
+    own_clip = cl[...]
     mk[0] = jnp.where(own_clip == cp[...], 1.0, 0.0)
     mk[1] = jnp.where(own_clip == cn[...], 1.0, 0.0)
 
@@ -195,46 +199,70 @@
         later = jnp.broadcast_to(mk[1, 0:1, 0:1], shape) > 0.5
         return before, later
 
-    def pick(own, index, r):
+    def pick_first(own, index, r):
+        before, _ = masks((ROWS, width))
+        lo = own[pl.ds(r, ROWS), :].astype(F32)
+        hi = own[pl.ds(half + r, ROWS), :].astype(F32)
+        return jnp.where(before, hi, lo)
+
+    def pick_second(own, index, r):
         before, later = masks((ROWS, width))
-        lo = own[pl.ds(r, ROWS), :].astype(F32)
         hi = own[pl.ds(half + r, ROWS), :].astype(F32)
         from_next = rn[index, pl.ds(r, ROWS), :].astype(F32)
         from_prev = rp[index, pl.ds(r, ROWS), :].astype(F32)
-        first = jnp.where(before, hi, lo)
-        second = jnp.where(later, from_next, jnp.where(before, from_prev, hi))
-        return first, second
+        return jnp.where(later, from_next, jnp.where(before, from_prev, hi))
 
     chunks = half // ROWS
 
-    def norm_rows(c, carry):
-        r = pl.multiple_of(c * ROWS, ROWS)
-        for base, rows in zip((0, half), pick(x_ref, 0, r)):
+    def norm_half(base, pick):
+        def norm_rows(c, carry):
+            r = pl.multiple_of(c * ROWS, ROWS)
+            rows = pick(x_ref, 0, r)
             at = pl.ds(base + r, ROWS)
             centered = rows - jnp.mean(rows, axis=-1, keepdims=True)
             inv = lax.rsqrt(jnp.mean(centered * centered, axis=-1, keepdims=True) + epsilon)
             normalized = centered * inv
             nz[at, :] = normalized
             iv[at, :] = jnp.broadcast_to(inv, (ROWS, 128))
-            nb[at, :] = (normalized * gain_ref[...]).astype(BF)
-        return carry
-
-    lax.fori_loop(0, chunks, norm_rows, 0)
-
+            nb[at, :] = (normalized * gn[...]).astype(BF)
+            return carry
+
+        lax.fori_loop(0, chunks, norm_rows, 0, unroll=2)
+
+    def project_half(base):
+        rows = pl.ds(base, half)
+
+        def project(j, carry):
+            proj[j, rows, :] = jnp.dot(nb[rows, :], w[j], preferred_element_type=F32).astype(BF)
+            return carry
+
+        lax.fori_loop(0, 3, project, 0)
+
+    def turn_half(base):
+        rows = pl.ds(base, half)
+        tr[pl.ds(0, width), :] = jnp.transpose(nb[rows, :].astype(F32))
+        for i in range(32):
+            nt[i % 2, (i // 2) % 2 * 2 + (i // 4) % 2, pl.ds(i // 8 * PAD, PAD), rows] = tr[
+                pl.ds(i * block, PAD), :
+            ].astype(BF)
+
+    norm_half(0, pick_first)
+    turn_half(0)
     for j in range(3):
         loads[j].wait()
-
-    def project(j, carry):
-        proj[j] = jnp.dot(nb[...], w[j], preferred_element_type=F32).astype(BF)
-        return carry
-
-    lax.fori_loop(0, 3, project, 0)
-
-    tr[pl.ds(0, width), :] = jnp.transpose(nb[...].astype(F32))
-    for i in range(32):
-        nt[i % 2, (i // 2) % 2 * 2 + (i // 4) % 2, pl.ds(i // 8 * PAD, PAD), :] = tr[
-            pl.ds(i * block, PAD), :
-        ].astype(BF)
+    project_half(0)
+
+    @pl.when(has_next)
+    def _():
+        x_p.wait_recv()
+
+    @pl.when(has_prev)
+    def _():
+        x_n.wait_recv()
+
+    norm_half(half, pick_second)
+    project_half(half)
+    turn_half(half)
     nt_copy = remote(6, nt.at[1 - core], nr, core_dev)
     nt_copy.start()
 
@@ -249,7 +277,7 @@
     def products(c, carry):
         r = pl.multiple_of(c * ROWS, ROWS)
         a, b = pl.ds(r, ROWS), pl.ds(half + r, ROWS)
-        do_a, do_b = pick(do_ref, 1, r)
+        do_a, do_b = pick_first(do_ref, 1, r), pick_second(do_ref, 1, r)
         dos[a, :] = do_a.astype(BF)
         dos[b, :] = do_b.astype(BF)
         kd = proj[1, a, :].astype(F32) - proj[1, b, :].astype(F32)
@@ -306,18 +334,28 @@
             nr[group], dvr[:, cols], preferred_element_type=F32
         )
 
-    cols_y, cols_x = pl.ds(0, SPLIT), pl.ds(SPLIT, width - SPLIT)
-
-    def send_terms(k, carry):
-        sx[k] = term((1 - xx) * 2 + k, cols_x).astype(BF)
-        sy[k] = term(k * 2 + (1 - y), cols_y).astype(BF)
-        return carry
-
-    lax.fori_loop(0, 2, send_terms, 0)
-    x_first = remote(10, sx, rx, x_dev)
-    y_first = remote(11, sy, ry, y_dev)
-    x_first.start()
-    y_first.start()
+    def in_y(k):
+        return pl.ds(*PARTS_Y[k])
+
+    def in_x(k):
+        return pl.ds(*PARTS_X[k])
+
+    def from_x(k):
+        return pl.ds(SPLIT + PARTS_X[k][0], PARTS_X[k][1])
+
+    x_first, y_first, x_second, y_second = [], [], [], []
+    for k in CHUNKS:
+
+        def send_terms(n, carry, k=k):
+            sx[n, :, in_x(k)] = term((1 - xx) * 2 + n, from_x(k)).astype(BF)
+            sy[n, :, in_y(k)] = term(n * 2 + (1 - y), in_y(k)).astype(BF)
+            return carry
+
+        lax.fori_loop(0, 2, send_terms, 0)
+        x_first.append(remote(10 + k, sx.at[:, :, in_x(k)], rx.at[:, :, in_x(k)], x_dev))
+        y_first.append(remote(13 + k, sy.at[:, :, in_y(k)], ry.at[:, :, in_y(k)], y_dev))
+        x_first[k].start()
+        y_first[k].start()
 
     def back(j, carry):
         part = lax.dot_general(
@@ -334,26 +372,20 @@
         at = pl.ds(r, ROWS)
         normalized, d_normed = nz[at, :], dn[at, :]
         prod = d_normed * normalized
-        d_hat = d_normed * gain_ref[...]
+        d_hat = d_normed * gn[...]
         first = jnp.mean(d_hat, axis=-1, keepdims=True)
         second = jnp.mean(d_hat * normalized, axis=-1, keepdims=True)
         result = iv[at, 0:1] * (d_hat - first - normalized * second)
         igs[at, :] = result.astype(BF)
         return acc + (prod[0:8] + prod[8:16])
 
-    gp[0] = lax.fori_loop(0, 2 * chunks, input_rows, jnp.zeros((8, width), F32))
+    gp[0] = lax.fori_loop(
+        0, 2 * chunks, input_rows, jnp.zeros((8, width), F32), unroll=2
+    )
 
     ig_p = remote(8, igs.at[upper], qn, prev)
     ig_n = remote(9, igs.at[upper], qp, after)
 
-    @pl.when(has_prev)
-    def _():
-        ig_p.start()
-
-    @pl.when(has_next)
-    def _():
-        ig_n.start()
-
     @pl.when(s == 0)
     def _():
         qp[...] = jnp.zeros_like(qp)
@@ -362,41 +394,74 @@
     def _():
         qn[...] = jnp.zeros_like(qn)
 
-    gain_core = remote(17, gp.at[0], gr.at[0], core_dev)
+    gain_core = remote(16, gp.at[0], gr.at[0], core_dev)
     gain_core.start()
 
-    def keep_terms(k, carry):
-        kx[k] = term(xx * 2 + k, cols_x)
-        ky[k] = term(k * 2 + y, cols_y)
+    def keep_terms(n, carry):
+        kx[n] = term(xx * 2 + n, pl.ds(SPLIT, width - SPLIT))
+        ky[n] = term(n * 2 + y, pl.ds(0, SPLIT))
         return carry
 
     lax.fori_loop(0, 2, keep_terms, 0)
 
     gain_core.wait_recv()
     gp[1] = gp[0] + gr[0]
-    gain_x = remote(18, gp.at[1], gr.at[1], x_dev)
+    gain_x = remote(17, gp.at[1], gr.at[1], x_dev)
     gain_x.start()
 
-    y_first.wait_recv()
-    tx[...] = (ky[1 - xx] + ry[1 - xx].astype(F32)).astype(BF)
-    x_second = remote(12, tx, rtx, x_dev)
-    x_second.start()
-    x_first.wait_recv()
-    ty[...] = (kx[1 - y] + rx[1 - y].astype(F32)).astype(BF)
-    y_second = remote(13, ty, rty, y_dev)
-    y_second.start()
+    for k in CHUNKS:
+        y_first[k].wait_recv()
+        tx[:, in_y(k)] = (
+            ky[1 - xx, :, in_y(k)] + ry[1 - xx, :, in_y(k)].astype(F32)
+        ).astype(BF)
+        x_second.append(remote(18 + k, tx.at[:, in_y(k)], rtx.at[:, in_y(k)], x_dev))
+        x_second[k].start()
+        x_first[k].wait_recv()
+        ty[:, in_x(k)] = (
+            kx[1 - y, :, in_x(k)] + rx[1 - y, :, in_x(k)].astype(F32)
+        ).astype(BF)
+        y_second.append(remote(21 + k, ty.at[:, in_x(k)], rty.at[:, in_x(k)], y_dev))
+        y_second[k].start()
+        fin[:, in_y(k)] = ky[xx, :, in_y(k)] + ry[xx, :, in_y(k)].astype(F32)
+        fin[:, from_x(k)] = kx[y, :, in_x(k)] + rx[y, :, in_x(k)].astype(F32)
+
+    @pl.when(has_prev)
+    def _():
+        ig_p.start()
+
+    @pl.when(has_next)
+    def _():
+        ig_n.start()
 
     gain_x.wait_recv()
     gp[2] = gp[1] + gr[1]
-    gain_y = remote(19, gp.at[2], gr.at[2], y_dev)
+    gain_y = remote(24, gp.at[2], gr.at[2], y_dev)
     gain_y.start()
 
-    fin[:, cols_y] = ky[xx] + ry[xx].astype(F32)
-    fin[:, cols_x] = kx[y] + rx[y].astype(F32)
+    z_copies = []
+
+    def pass_on(index, cols):
+        for n in range(4):
+            u[n, :, cols] = fin[pl.ds(n * PAD, PAD), cols].astype(BF)
+        for d in range(3):
+            z_copies.append(
+                remote(
+                    index + d, u.at[lax.rem(z + d + 1, 4), :, cols], zr.at[d, :, cols], z_devs[d]
+                )
+            )
+            z_copies[-1].start()
+
+    for k in CHUNKS:
+        y_second[k].wait_recv()
+        fin[:, from_x(k)] = fin[:, from_x(k)] + rty[:, in_x(k)].astype(F32)
+        pass_on(28 + 6 * k, from_x(k))
+        x_second[k].wait_recv()
+        fin[:, in_y(k)] = fin[:, in_y(k)] + rtx[:, in_y(k)].astype(F32)
+        pass_on(31 + 6 * k, in_y(k))
 
     gain_y.wait_recv()
     zg[z] = gp[2] + gr[2]
-    gain_z = [remote(20 + d, zg.at[z], zg.at[z], z_devs[d]) for d in range(3)]
+    gain_z = [remote(25 + d, zg.at[z], zg.at[z], z_devs[d]) for d in range(3)]
     for copy in gain_z:
         copy.start()
 
@@ -421,23 +486,11 @@
 
     lax.fori_loop(0, chunks, output_rows, 0)
 
-    x_second.wait_recv()
-    fin[:, cols_y] = fin[:, cols_y] + rtx[...].astype(F32)
-    y_second.wait_recv()
-    fin[:, cols_x] = fin[:, cols_x] + rty[...].astype(F32)
-    for k in range(4):
-        u[k] = fin[pl.ds(k * PAD, PAD), :].astype(BF)
-    z_copies = [
-        remote(14 + d, u.at[lax.rem(z + d + 1, 4)], zr.at[d], z_devs[d]) for d in range(3)
-    ]
-    for copy in z_copies:
-        copy.start()
-
     factor = (x_ref.shape[0] * 32) ** (-0.5)
     for copy in gain_z:
         copy.wait_recv()
     total = (zg[0] + zg[1]) + (zg[2] + zg[3])
-    gg_ref[...] = jnp.sum(total, axis=0, keepdims=True) * factor
+    gg_ref[...] = jnp.sum(total, axis=0) * factor
 
     for copy in z_copies:
         copy.wait_recv()
@@ -455,16 +508,27 @@
         for copy in to_next + [ig_n]:
             copy.wait_send()
 
-    sent = [nt_copy, dv_copy, x_first, y_first, x_second, y_second, gain_core, gain_x, gain_y]
-    for copy in sent + gain_z + z_copies:
+    sent = [nt_copy, dv_copy, gain_core, gain_x, gain_y] + x_first + y_first
+    for copy in sent + x_second + y_second + gain_z + z_copies:
         copy.wait_send()
+
+
+def settle(a, b, c, a_out, b_out, c_out, sem):
+    copies = [
+        pltpu.make_async_copy(src, dst, sem.at[i])
+        for i, (src, dst) in enumerate(((a, a_out), (b, b_out), (c, c_out)))
+    ]
+    for copy in copies:
+        copy.start()
+    for copy in copies:
+        copy.wait()
 
 
 def paired_shards(block_input, norm_gain, qkv_weight, frame_clip, out_grad):
     tokens, width = block_input.shape[2:]
     half = tokens // 2
     block = width // 32
-    clip = jnp.broadcast_to(frame_clip.astype(F32), (8, 128))
+    smem = pl.BlockSpec(memory_space=pltpu.SMEM)
     vmem = pl.BlockSpec(memory_space=pltpu.VMEM)
     rest = width - SPLIT
     group = 4 * PAD
@@ -472,17 +536,20 @@
     def buf(*shape):
         return pltpu.VMEM(shape, BF)
 
+    def ids(*shape):
+        return pltpu.VMEM(shape, jnp.int32)
+
     def wide(*shape):
         return pltpu.VMEM(shape, F32)
 
     scratch = [
-        buf(3, width, width), buf(2, half, width), buf(2, half, width),
-        wide(8, 128), wide(8, 128), wide(2, 8, 128),
+        wide(1, width), ids(8, 128), buf(3, width, width), buf(2, half, width), buf(2, half, width),
+        ids(8, 128), ids(8, 128), wide(2, 8, 128),
         wide(tokens, width), wide(tokens, 128), buf(tokens, width), buf(tokens, width),
         buf(3, tokens, width), buf(tokens, width), buf(tokens, width),
         buf(width, 128), buf(128, width), buf(3, tokens, width), buf(3, tokens, width),
         wide(tokens, width), buf(tokens, width), buf(half, width), buf(half, width),
-        wide(width + 8, tokens), buf(2, 4, group, tokens), buf(4, group, tokens),
+        wide(width + 8, half), buf(2, 4, group, tokens), buf(4, group, tokens),
         buf(tokens, width),
         buf(2, group, rest), buf(2, group, SPLIT), buf(2, group, rest), buf(2, group, SPLIT),
         wide(2, group, rest), wide(2, group, SPLIT),
@@ -490,16 +557,16 @@
         wide(group, width), buf(4, PAD, width), buf(3, PAD, width),
         wide(3, 8, width), wide(3, 8, width), wide(4, 8, width),
         pltpu.SemaphoreType.DMA((3,)),
-        pltpu.SemaphoreType.DMA((23,)), pltpu.SemaphoreType.DMA((23,)),
+        pltpu.SemaphoreType.DMA((46,)), pltpu.SemaphoreType.DMA((46,)),
     ]
-    input_grad, weight_grad, gain_grad = pl.pallas_call(
+    results = pl.pallas_call(
         fused,
         out_shape=(
             jax.ShapeDtypeStruct((tokens, width), BF),
             jax.ShapeDtypeStruct((block, width), F32),
-            jax.ShapeDtypeStruct((1, width), F32),
+            jax.ShapeDtypeStruct((width,), F32),
         ),
-        in_specs=[vmem, vmem, vmem, pl.BlockSpec(memory_space=pl.ANY), vmem],
+        in_specs=[vmem, vmem, vmem, pl.BlockSpec(memory_space=pl.ANY), smem],
         out_specs=(vmem, vmem, vmem),
         scratch_shapes=scratch,
         compiler_params=pltpu.CompilerParams(
@@ -508,8 +575,16 @@
         cost_estimate=pl.CostEstimate(
             flops=8_000_000_000, bytes_accessed=16_000_000, transcendentals=100_000
         ),
-    )(block_input[0, 0], out_grad[0, 0], norm_gain[None], qkv_weight, clip)
-    return input_grad[None, None], weight_grad, gain_grad[0]
+    )(block_input[0, 0], out_grad[0, 0], norm_gain, qkv_weight, frame_clip)
+    any_place = pl.BlockSpec(memory_space=pl.ANY)
+    input_grad, weight_grad, gain_grad = pl.pallas_call(
+        settle,
+        out_shape=tuple(jax.ShapeDtypeStruct(r.shape, r.dtype) for r in results),
+        in_specs=[any_place] * 3,
+        out_specs=(any_place,) * 3,
+        scratch_shapes=[pltpu.SemaphoreType.DMA((3,))],
+    )(*results)
+    return input_grad[None, None], weight_grad, gain_grad
 
 
 def solution(mesh):

time: 69.7 us -> 89.5 us (1.28)
  the two profiles are of different devices: /device:TPU:14 before, /device:TPU:3 now
where the time goes in v2:
time: 89.5 us; the launch traced here: 89.3 us
  Pallas kernels  88 us (98%)
  between operations  1.29 us (1%)
    pallas_call x1, Pallas kernels, paired_shards(): pl.pallas_call(fused, out_shape=(jax.ShapeDtypeStruct((tokens, width), BF...  56.7 us
    pallas_call x1, Pallas kernels, paired_shards(): pl.pallas_call(settle, out_shape=tuple((jax.ShapeDtypeStruct(r.shape, r.d...  31.3 us

profile of v2, /device:TPU:3, one launch (start us, length us, event | category | flops | bytes accessed | tf_op | source)
XLA Modules:
  0.0 89.3 jit_solution(9720019097124620695)
XLA Ops:
  1.3 56.7 %shard_map.76 = (bf16[256,1408]{1,0:T(8,128)(2,1)}, f32[44,1408]{1,0:T(8,128)}, f32[1408]{0:T(1024)}) custom-call(bf16[256,1408]{1,0:T(8,128)(2,1)} %bitcast.3, bf16[256,1408]{1,0:T(8,128)(2,1)} %bitcast.4, f32[1408]{0:T(1024)} %gain_ref.1, bf16[1408,4224]{1,0:T(8,128)(2,1)} %w_hbm.1, s32[1,1]{1,0:T(1,128)S(6)} %copy.8.clip_ref), custom_call_target="tpu_custom_call" | custom-call | flops 8000000000 | bytes 16000000 | tf_op jit(solution)/shard_map/pallas_call | solution.py:562
  58.0 31.3 %shard_map.77 = (bf16[256,1408]{1,0:T(8,128)(2,1)}, f32[44,1408]{1,0:T(8,128)}, f32[1408]{0:T(1024)}) custom-call(bf16[256,1408]{1,0:T(8,128)(2,1)} %get-tuple-element.9.a, f32[44,1408]{1,0:T(8,128)} %get-tuple-element.10.b, f32[1408]{0:T(1024)} %get-tuple-element.11.c), custom_call_target="tpu_custom_call" | custom-call | tf_op jit(solution)/shard_map/pallas_call | solution.py:580

commit v3 on v2

--- a/solution.py
+++ b/solution.py
@@ -104,7 +104,7 @@
 def fused(
     x_ref, do_ref, gain_ref, w_hbm, clip_ref,
     ig_ref, wg_ref, gg_ref,
-    gn, cl, w, rn, rp, cn, cp, mk, nz, iv, nb, dos, proj, t1, t2, em, et, bc, g, dn, igs, qn, qp,
+    gn, cl, w, rn, rp, cn, cp, mk, nz, iv, nb, dos, proj, t1, t2, em, et, bc, g, dn, dnt, igs, qn, qp,
     tr, nt, nr, dvr, sx, sy, rx, ry, kx, ky, tx, ty, rtx, rty, fin, u, zr, gp, gr, zg,
     wsem, send, recv,
 ):
@@ -357,46 +357,6 @@
         x_first[k].start()
         y_first[k].start()
 
-    def back(j, carry):
-        part = lax.dot_general(
-            g[j], w[j], (((1,), (1,)), ((), ())), preferred_element_type=F32
-        )
-        dn[...] = dn[...] + part
-        return carry
-
-    dn[...] = jnp.zeros_like(dn)
-    lax.fori_loop(0, 3, back, 0)
-
-    def input_rows(c, acc):
-        r = pl.multiple_of(c * ROWS, ROWS)
-        at = pl.ds(r, ROWS)
-        normalized, d_normed = nz[at, :], dn[at, :]
-        prod = d_normed * normalized
-        d_hat = d_normed * gn[...]
-        first = jnp.mean(d_hat, axis=-1, keepdims=True)
-        second = jnp.mean(d_hat * normalized, axis=-1, keepdims=True)
-        result = iv[at, 0:1] * (d_hat - first - normalized * second)
-        igs[at, :] = result.astype(BF)
-        return acc + (prod[0:8] + prod[8:16])
-
-    gp[0] = lax.fori_loop(
-        0, 2 * chunks, input_rows, jnp.zeros((8, width), F32), unroll=2
-    )
-
-    ig_p = remote(8, igs.at[upper], qn, prev)
-    ig_n = remote(9, igs.at[upper], qp, after)
-
-    @pl.when(s == 0)
-    def _():
-        qp[...] = jnp.zeros_like(qp)
-
-    @pl.when(s == 3)
-    def _():
-        qn[...] = jnp.zeros_like(qn)
-
-    gain_core = remote(16, gp.at[0], gr.at[0], core_dev)
-    gain_core.start()
-
     def keep_terms(n, carry):
         kx[n] = term(xx * 2 + n, pl.ds(SPLIT, width - SPLIT))
         ky[n] = term(n * 2 + y, pl.ds(0, SPLIT))
@@ -404,12 +364,13 @@
 
     lax.fori_loop(0, 2, keep_terms, 0)
 
-    gain_core.wait_recv()
-    gp[1] = gp[0] + gr[0]
-    gain_x = remote(17, gp.at[1], gr.at[1], x_dev)
-    gain_x.start()
-
-    for k in CHUNKS:
+    def back(j):
+        part = lax.dot_general(
+            w[j], g[j], (((1,), (1,)), ((), ())), preferred_element_type=F32
+        )
+        dnt[...] = part if j == 0 else dnt[...] + part
+
+    def second_stage(k):
         y_first[k].wait_recv()
         tx[:, in_y(k)] = (
             ky[1 - xx, :, in_y(k)] + ry[1 - xx, :, in_y(k)].astype(F32)
@@ -425,19 +386,6 @@
         fin[:, in_y(k)] = ky[xx, :, in_y(k)] + ry[xx, :, in_y(k)].astype(F32)
         fin[:, from_x(k)] = kx[y, :, in_x(k)] + rx[y, :, in_x(k)].astype(F32)
 
-    @pl.when(has_prev)
-    def _():
-        ig_p.start()
-
-    @pl.when(has_next)
-    def _():
-        ig_n.start()
-
-    gain_x.wait_recv()
-    gp[2] = gp[1] + gr[1]
-    gain_y = remote(24, gp.at[2], gr.at[2], y_dev)
-    gain_y.start()
-
     z_copies = []
 
     def pass_on(index, cols):
@@ -451,13 +399,76 @@
             )
             z_copies[-1].start()
 
-    for k in CHUNKS:
+    def finish(k):
         y_second[k].wait_recv()
         fin[:, from_x(k)] = fin[:, from_x(k)] + rty[:, in_x(k)].astype(F32)
         pass_on(28 + 6 * k, from_x(k))
         x_second[k].wait_recv()
         fin[:, in_y(k)] = fin[:, in_y(k)] + rtx[:, in_y(k)].astype(F32)
         pass_on(31 + 6 * k, in_y(k))
+
+    back(0)
+    second_stage(0)
+    back(1)
+    back(2)
+    dn[...] = jnp.transpose(dnt[...])
+
+    def input_rows(c, acc):
+        r = pl.multiple_of(c * ROWS, ROWS)
+        at = pl.ds(r, ROWS)
+        normalized, d_normed = nz[at, :], dn[at, :]
+        prod = d_normed * normalized
+        d_hat = d_normed * gn[...]
+        first = jnp.mean(d_hat, axis=-1, keepdims=True)
+        second = jnp.mean(d_hat * normalized, axis=-1, keepdims=True)
+        result = iv[at, 0:1] * (d_hat - first - normalized * second)
+        igs[at, :] = result.astype(BF)
+        return acc + (prod[0:8] + prod[8:16])
+
+    gp[0] = lax.fori_loop(
+        0, 2 * chunks, input_rows, jnp.zeros((8, width), F32), unroll=2
+    )
+
+    ig_p = remote(8, igs.at[upper], qn, prev)
+    ig_n = remote(9, igs.at[upper], qp, after)
+
+    @pl.when(s == 0)
+    def _():
+        qp[...] = jnp.zeros_like(qp)
+
+    @pl.when(s == 3)
+    def _():
+        qn[...] = jnp.zeros_like(qn)
+
+    gain_core = remote(16, gp.at[0], gr.at[0], core_dev)
+    gain_core.start()
+
+    second_stage(1)
+    finish(0)
+
+    gain_core.wait_recv()
+    gp[1] = gp[0] + gr[0]
+    gain_x = remote(17, gp.at[1], gr.at[1], x_dev)
+    gain_x.start()
+
+    second_stage(2)
+
+    @pl.when(has_prev)
+    def _():
+        ig_p.start()
+
+    @pl.when(has_next)
+    def _():
+        ig_n.start()
+
+    finish(1)
+
+    gain_x.wait_recv()
+    gp[2] = gp[1] + gr[1]
+    gain_y = remote(24, gp.at[2], gr.at[2], y_dev)
+    gain_y.start()
+
+    finish(2)
 
     gain_y.wait_recv()
     zg[z] = gp[2] + gr[2]
@@ -513,15 +524,10 @@
         copy.wait_send()
 
 
-def settle(a, b, c, a_out, b_out, c_out, sem):
-    copies = [
-        pltpu.make_async_copy(src, dst, sem.at[i])
-        for i, (src, dst) in enumerate(((a, a_out), (b, b_out), (c, c_out)))
-    ]
-    for copy in copies:
-        copy.start()
-    for copy in copies:
-        copy.wait()
+def settle(a, b, c, a_out, b_out, c_out):
+    a_out[...] = a[...]
+    b_out[...] = b[...]
+    c_out[...] = c[...]
 
 
 def paired_shards(block_input, norm_gain, qkv_weight, frame_clip, out_grad):
@@ -548,7 +554,8 @@
         wide(tokens, width), wide(tokens, 128), buf(tokens, width), buf(tokens, width),
         buf(3, tokens, width), buf(tokens, width), buf(tokens, width),
         buf(width, 128), buf(128, width), buf(3, tokens, width), buf(3, tokens, width),
-        wide(tokens, width), buf(tokens, width), buf(half, width), buf(half, width),
+        wide(tokens, width), wide(width, tokens), buf(tokens, width),
+        buf(half, width), buf(half, width),
         wide(width + 8, half), buf(2, 4, group, tokens), buf(4, group, tokens),
         buf(tokens, width),
         buf(2, group, rest), buf(2, group, SPLIT), buf(2, group, rest), buf(2, group, SPLIT),
@@ -576,13 +583,11 @@
             flops=8_000_000_000, bytes_accessed=16_000_000, transcendentals=100_000
         ),
     )(block_input[0, 0], out_grad[0, 0], norm_gain, qkv_weight, frame_clip)
-    any_place = pl.BlockSpec(memory_space=pl.ANY)
     input_grad, weight_grad, gain_grad = pl.pallas_call(
         settle,
         out_shape=tuple(jax.ShapeDtypeStruct(r.shape, r.dtype) for r in results),
-        in_specs=[any_place] * 3,
-        out_specs=(any_place,) * 3,
-        scratch_shapes=[pltpu.SemaphoreType.DMA((3,))],
+        in_specs=[vmem] * 3,
+        out_specs=(vmem,) * 3,
     )(*results)
     return input_grad[None, None], weight_grad, gain_grad
 

time: 89.5 us -> 60.3 us (0.67)
  Pallas kernels: 88 us -> 58.9 us
    pallas_call x1, Pallas kernels: 31.3 us -> 2.17 us  [paired_shards(): pl.pallas_call(settle, out_shape=tuple((jax.ShapeDtypeStruct(r.shape, r.d...]
where the time goes in v3:
time: 60.3 us; the launch traced here: 60.2 us
  Pallas kernels  58.9 us (98%)
  between operations  1.29 us (2%)
    pallas_call x1, Pallas kernels, paired_shards(): pl.pallas_call(fused, out_shape=(jax.ShapeDtypeStruct((tokens, width), BF...  56.7 us
    pallas_call x1, Pallas kernels, paired_shards(): pl.pallas_call(settle, out_shape=tuple((jax.ShapeDtypeStruct(r.shape, r.d...  2.17 us

profile of v3, /device:TPU:3, one launch (start us, length us, event | category | flops | bytes accessed | tf_op | source)
XLA Modules:
  0.0 60.2 jit_solution(2824125059859106691)
XLA Ops:
  1.3 56.7 %shard_map.76 = (bf16[256,1408]{1,0:T(8,128)(2,1)}, f32[44,1408]{1,0:T(8,128)}, f32[1408]{0:T(1024)}) custom-call(bf16[256,1408]{1,0:T(8,128)(2,1)} %bitcast.3, bf16[256,1408]{1,0:T(8,128)(2,1)} %bitcast.4, f32[1408]{0:T(1024)} %gain_ref.1, bf16[1408,4224]{1,0:T(8,128)(2,1)} %w_hbm.1, s32[1,1]{1,0:T(1,128)S(6)} %copy.8.clip_ref), custom_call_target="tpu_custom_call" | custom-call | flops 8000000000 | bytes 16000000 | tf_op jit(solution)/shard_map/pallas_call | solution.py:569
  58.0 2.2 %shard_map.77 = (bf16[256,1408]{1,0:T(8,128)(2,1)}, f32[44,1408]{1,0:T(8,128)}, f32[1408]{0:T(1024)}) custom-call(bf16[256,1408]{1,0:T(8,128)(2,1)} %get-tuple-element.9.a, f32[44,1408]{1,0:T(8,128)} %get-tuple-element.10.b, f32[1408]{0:T(1024)} %get-tuple-element.11.c), custom_call_target="tpu_custom_call" | custom-call | tf_op jit(solution)/shard_map/pallas_call | solution.py:586

commit v4 on v3

--- a/solution.py
+++ b/solution.py
@@ -443,6 +443,14 @@
     gain_core = remote(16, gp.at[0], gr.at[0], core_dev)
     gain_core.start()
 
+    @pl.when(has_prev)
+    def _():
+        ig_p.start()
+
+    @pl.when(has_next)
+    def _():
+        ig_n.start()
+
     second_stage(1)
     finish(0)
 
@@ -452,14 +460,6 @@
     gain_x.start()
 
     second_stage(2)
-
-    @pl.when(has_prev)
-    def _():
-        ig_p.start()
-
-    @pl.when(has_next)
-    def _():
-        ig_n.start()
 
     finish(1)
 

time: 60.3 us -> 60.3 us (level)
  no operation moved by 1% of the time
where the time goes in v4:
time: 60.3 us; the launch traced here: 60.2 us
  Pallas kernels  58.9 us (98%)
  between operations  1.29 us (2%)
    pallas_call x1, Pallas kernels, paired_shards(): pl.pallas_call(fused, out_shape=(jax.ShapeDtypeStruct((tokens, width), BF...  56.7 us
    pallas_call x1, Pallas kernels, paired_shards(): pl.pallas_call(settle, out_shape=tuple((jax.ShapeDtypeStruct(r.shape, r.d...  2.17 us

profile of v4, /device:TPU:3, one launch (start us, length us, event | category | flops | bytes accessed | tf_op | source)
XLA Modules:
  0.0 60.2 jit_solution(3771004082613365315)
XLA Ops:
  1.3 56.7 %shard_map.76 = (bf16[256,1408]{1,0:T(8,128)(2,1)}, f32[44,1408]{1,0:T(8,128)}, f32[1408]{0:T(1024)}) custom-call(bf16[256,1408]{1,0:T(8,128)(2,1)} %bitcast.3, bf16[256,1408]{1,0:T(8,128)(2,1)} %bitcast.4, f32[1408]{0:T(1024)} %gain_ref.1, bf16[1408,4224]{1,0:T(8,128)(2,1)} %w_hbm.1, s32[1,1]{1,0:T(1,128)S(6)} %copy.8.clip_ref), custom_call_target="tpu_custom_call" | custom-call | flops 8000000000 | bytes 16000000 | tf_op jit(solution)/shard_map/pallas_call | solution.py:569
  58.0 2.2 %shard_map.77 = (bf16[256,1408]{1,0:T(8,128)(2,1)}, f32[44,1408]{1,0:T(8,128)}, f32[1408]{0:T(1024)}) custom-call(bf16[256,1408]{1,0:T(8,128)(2,1)} %get-tuple-element.9.a, f32[44,1408]{1,0:T(8,128)} %get-tuple-element.10.b, f32[1408]{0:T(1024)} %get-tuple-element.11.c), custom_call_target="tpu_custom_call" | custom-call | tf_op jit(solution)/shard_map/pallas_call | solution.py:586
